TPU v7x, 32 devices: a whole 2x2x4 slice. The times are simulated.
32 devices in a mesh: grp: 2 (over x), ctx: 16 (over z, y, core).
Axes of the slice: x: 2, y: 2, z: 4, core: 2. Of those that a mesh axis runs over, the one named last changes fastest.
Arguments:
- seq_feats: bfloat16 [16384, 768], P(('grp', 'ctx')), may hold values from -6 to 6
- taps: float32 [7, 768], replicated, may hold values from -2 to 2
- pole_table: float32 [64], replicated, may hold values from 30 to 65536
- mode_index: int32 [256, 16], P(('grp', 'ctx')), may hold values from 0 to 63
- residues: float32 [256, 16], P(('grp', 'ctx')), may hold values from -1.5 to 1.5
- skip: float32 [256], P(('grp', 'ctx')), may hold values from 0.5 to 1.5
Outputs:
- mixer_out: bfloat16 [16384, 256], P(('grp', 'ctx'))
All inputs are finite; a program needn't handle non-finite values.
Results may differ from a plain program's by a relative error of at most 0.005.
Values may be sent and summed in bfloat16 or wider, within the bound.
A program may use at most 128 MiB of HBM per device.

v0:
```python
import functools

import jax
import jax.numpy as jnp
from jax import lax
from jax.experimental import pallas as pl
from jax.experimental.pallas import tpu as pltpu
from jax.sharding import PartitionSpec as P

F32 = jnp.float32
BF16 = jnp.bfloat16
CHUNK = 32
ROWS = 64
COLS = 256
MESH = pl.DeviceIdType.MESH


def upper(value):
    return value.astype(BF16).astype(F32)


def paired(value, poles):
    high = upper(value)
    lane = lax.broadcasted_iota(jnp.int32, value.shape, 1)
    both = jnp.where(lane < poles, high, value - high).astype(BF16)
    return jnp.concatenate([both, both], axis=1)


def dot_last(left, right):
    return lax.dot_general(left, right, (((1,), (1,)), ((), ())), preferred_element_type=F32)


def kernel(
    outer, inner, x_ref, taps_ref, pole_ref, mode_ref, res_ref, skip_ref, out_ref,
    halo, wall, wsend, state, landed, turned, incoming,
    xs, gs, gb, grid, ys, qs, filt, acat, bcat, fcat, short,
    halo_send, halo_recv, w_send, w_recv, s_send, s_recv, x_send, x_recv,
):
    count = outer * inner
    tok, width3 = x_ref.shape
    chans = width3 // 3
    ntaps = taps_ref.shape[0]
    poles = pole_ref.shape[1]
    own, modes = mode_ref.shape
    seq = tok * count
    nchunk = tok // CHUNK
    me = lax.axis_index("grp") * inner + lax.axis_index("ctx")

    def where_is(index):
        return {"grp": index // inner, "ctx": lax.rem(index, inner)}

    barrier = pltpu.get_barrier_semaphore()

    def greet(step, carry):
        peer = lax.rem(me + step, count)
        pl.semaphore_signal(barrier, inc=1, device_id=where_is(peer), device_id_type=MESH)
        return carry

    lax.fori_loop(1, count, greet, 0)

    pole = jnp.concatenate([pole_ref[...], pole_ref[...]], axis=1)
    small = -2.0 / pole
    series = small * (1.0 + small * (0.5 + small * (1.0 / 6 + small * (1.0 / 24 + small * (
        1.0 / 120 + small * (1.0 / 720))))))
    energy = (jnp.exp(-2.0 * seq / pole) - 1.0) / series
    lane = lax.broadcasted_iota(jnp.int32, (own, 2 * poles), 1)
    entry = lax.rem(lane, poles)
    weight = jnp.zeros((own, 2 * poles), F32)
    for mode in range(modes):
        weight += jnp.where(mode_ref[:, mode : mode + 1] == entry, res_ref[:, mode : mode + 1], 0.0)
    weight = weight / jnp.sqrt(energy)
    diag = lax.broadcasted_iota(jnp.int32, (own, own), 0) == lax.broadcasted_iota(jnp.int32, (own, own), 1)
    skip_col = jnp.sum(jnp.where(diag, skip_ref[...], 0.0), axis=1, keepdims=True)
    mine = pl.ds(pl.multiple_of(me * own, own), own)
    wsend[...] = jnp.where(lane < poles, weight, jnp.where(lane == poles, skip_col, 0.0))
    wall[mine, :] = wsend[...]

    pl.semaphore_wait(barrier, count - 1)

    halo_copy = pltpu.make_async_remote_copy(
        src_ref=x_ref.at[tok - 16 :], dst_ref=halo, send_sem=halo_send, recv_sem=halo_recv,
        device_id=where_is(lax.rem(me + 1, count)), device_id_type=MESH,
    )

    @pl.when(me < count - 1)
    def _():
        halo_copy.start()

    @pl.when(me == 0)
    def _():
        halo[...] = jnp.zeros_like(halo)

    def push_weight(step, carry):
        peer = lax.rem(me + step, count)
        pltpu.make_async_remote_copy(
            src_ref=wsend, dst_ref=wall.at[mine, :], send_sem=w_send, recv_sem=w_recv,
            device_id=where_is(peer), device_id_type=MESH,
        ).start()
        return carry

    lax.fori_loop(1, count, push_weight, 0)

    square = lax.broadcasted_iota(jnp.int32, (poles, poles), 0) == lax.broadcasted_iota(
        jnp.int32, (poles, poles), 1)
    column = jnp.sum(jnp.where(square, pole_ref[...], 0.0), axis=1, keepdims=True)

    def ending(length):
        back = (length - 1 - lax.broadcasted_iota(jnp.int32, (poles, length), 1)).astype(F32)
        table = jnp.exp(-back / column)
        high = upper(table)
        return jnp.concatenate([high.astype(BF16), (table - high).astype(BF16)], axis=0)

    def starting(length, first):
        ahead = (first + lax.broadcasted_iota(jnp.int32, (length, 2 * poles), 0)).astype(F32)
        table = jnp.exp(-ahead / pole)
        high = upper(table)
        return jnp.concatenate([high.astype(BF16), (table - high).astype(BF16)], axis=1)

    acat[...] = ending(tok)
    short[...] = ending(CHUNK)
    bcat[...] = starting(tok, 1)
    fcat[...] = starting(CHUNK, 0)

    def fir(block, col):
        rows = xs[pl.ds(pl.multiple_of(block * ROWS, ROWS), ROWS + 8), col : col + COLS]
        total = jnp.zeros((ROWS, COLS), F32)
        for tap in range(ntaps):
            total += taps_ref[tap : tap + 1, col : col + COLS] * rows[8 - tap : 8 - tap + ROWS]
        return total

    def gate(block, carry):
        place = pl.ds(pl.multiple_of(block * ROWS, ROWS), ROWS)
        for col in range(0, chans, COLS):
            low = (fir(block, chans + col) * fir(block, 2 * chans + col)).astype(BF16)
            gb[place, col : col + COLS] = low
            wide = low.astype(F32)
            for part in range(0, COLS, 128):
                gs[(col + part) // 128, place, :] = wide[:, part : part + 128]
        return carry

    xs[8:, :] = x_ref[...].astype(F32)
    lax.fori_loop(1, tok // ROWS, gate, 0)

    @pl.when(me > 0)
    def _():
        halo_copy.wait_recv()

    xs[0:8, :] = halo[...].astype(F32)[8:16]
    gate(0, 0)

    state[...] = jnp.dot(acat[...], gb[...], preferred_element_type=F32).T
    landed[me] = state[mine, :]

    def push_state(step, carry):
        peer = lax.rem(me + step, count)
        pltpu.make_async_remote_copy(
            src_ref=state.at[pl.ds(pl.multiple_of(peer * own, own), own), :], dst_ref=landed.at[me],
            send_sem=s_send, recv_sem=s_recv,
            device_id=where_is(peer), device_id_type=MESH,
        ).start()
        return carry

    lax.fori_loop(1, count, push_state, 0)

    def query(block, carry):
        place = pl.ds(pl.multiple_of(block * ROWS, ROWS), ROWS)
        for col in range(0, chans, COLS):
            qs[place, col : col + COLS] = fir(block, col)
        return carry

    lax.fori_loop(0, tok // ROWS, query, 0)

    others = (count - 1) * own
    pltpu.make_async_copy(wall.at[0:others, :], wall.at[0:others, :], w_recv).wait()
    lane_all = lax.broadcasted_iota(jnp.int32, (chans, 2 * poles), 1)
    gathered = wall[...]
    twice = jnp.where(lane_all < poles, gathered, pltpu.roll(gathered, poles, 1))
    across = gathered.T
    by_pole = across[0:poles]
    first_row = lax.broadcasted_iota(jnp.int32, (CHUNK, chans), 0) == 0
    filt[...] = dot_last(fcat[...], paired(twice, poles)) + jnp.where(
        first_row, across[poles : poles + 1], 0.0)

    grid[0:CHUNK] = jnp.zeros((CHUNK, nchunk, chans), F32)
    for pos in range(CHUNK):
        for col in range(0, chans, 128):
            grid[CHUNK + pos, :, col : col + 128] = gs[col // 128, pl.ds(pos, nchunk, stride=CHUNK), :]

    def within(pos, carry):
        for col in range(0, chans, 128):
            total = jnp.zeros((nchunk, 128), F32)
            for lag in range(CHUNK):
                total += filt[lag : lag + 1, col : col + 128] * grid[CHUNK + pos - lag, :, col : col + 128]
            ys[col // 128, pl.ds(pos, nchunk, stride=CHUNK), :] = total
        return carry

    lax.fori_loop(0, CHUNK, within, 0)

    all_but_one = landed.at[0 : count - 1]
    pltpu.make_async_copy(all_but_one, all_but_one, s_recv).wait()
    jump = jnp.exp(-float(tok) / pole)
    running = jnp.zeros((own, 2 * poles), F32)
    for source in range(count):
        turned[source] = running * weight
        part = landed[source]
        running = running * jump + (part + pltpu.roll(part, poles, 1))
    incoming[mine, :] = turned[me]

    def push_turned(step, carry):
        peer = lax.rem(me + step, count)
        pltpu.make_async_remote_copy(
            src_ref=turned.at[peer], dst_ref=incoming.at[mine, :], send_sem=x_send, recv_sem=x_recv,
            device_id=where_is(peer), device_id_type=MESH,
        ).start()
        return carry

    lax.fori_loop(1, count, push_turned, 0)

    hop = jnp.exp(-float(CHUNK) / column)

    def between(chunk, carried):
        place = pl.ds(pl.multiple_of(chunk * CHUNK, CHUNK), CHUNK)
        high = carried.astype(BF16)
        low = (carried - high.astype(F32)).astype(BF16)
        stack = jnp.concatenate([high, low, high, low], axis=0)
        entering = jnp.dot(bcat[0:CHUNK, :], stack, preferred_element_type=F32)
        for col in range(0, chans, 128):
            ys[col // 128, place, :] += entering[:, col : col + 128]
        fresh = jnp.dot(short[...], gb[place, :], preferred_element_type=F32)
        return carried * hop + by_pole * (fresh[0:poles] + fresh[poles:])

    lax.fori_loop(0, nchunk, between, jnp.zeros((poles, chans), F32))

    pltpu.make_async_copy(incoming.at[0:others, :], incoming.at[0:others, :], x_recv).wait()
    stack = paired(incoming[...], poles)
    for row in range(0, tok, 128):
        conv = dot_last(bcat[row : row + 128, :], stack)
        for col in range(0, chans, 128):
            mixed = conv[:, col : col + 128] + ys[col // 128, row : row + 128, :]
            out_ref[row : row + 128, col : col + 128] = (
                qs[row : row + 128, col : col + 128] * mixed).astype(BF16)

    @pl.when(me < count - 1)
    def _():
        halo_copy.wait_send()

    pltpu.make_async_copy(wall.at[0:others, :], wall.at[0:others, :], w_send).wait()
    pltpu.make_async_copy(all_but_one, all_but_one, s_send).wait()
    pltpu.make_async_copy(incoming.at[0:others, :], incoming.at[0:others, :], x_send).wait()


def body(seq_feats, taps, pole_table, mode_index, residues, skip):
    tok, width3 = seq_feats.shape
    chans = width3 // 3
    outer = lax.axis_size("grp")
    inner = lax.axis_size("ctx")
    count = outer * inner
    poles = pole_table.shape[0]
    own = mode_index.shape[0]
    nchunk = tok // CHUNK
    vmem = pl.BlockSpec(memory_space=pltpu.VMEM)
    sem = pltpu.SemaphoreType.DMA
    return pl.pallas_call(
        functools.partial(kernel, outer, inner),
        out_shape=jax.ShapeDtypeStruct((tok, chans), BF16),
        in_specs=[vmem] * 6,
        out_specs=vmem,
        scratch_shapes=[
            pltpu.VMEM((16, width3), BF16),
            pltpu.VMEM((chans, 2 * poles), F32),
            pltpu.VMEM((own, 2 * poles), F32),
            pltpu.VMEM((chans, 2 * poles), F32),
            pltpu.VMEM((count, own, 2 * poles), F32),
            pltpu.VMEM((count, own, 2 * poles), F32),
            pltpu.VMEM((chans, 2 * poles), F32),
            pltpu.VMEM((tok + 8, width3), F32),
            pltpu.VMEM((chans // 128, tok, 128), F32),
            pltpu.VMEM((tok, chans), BF16),
            pltpu.VMEM((2 * CHUNK, nchunk, chans), F32),
            pltpu.VMEM((chans // 128, tok, 128), F32),
            pltpu.VMEM((tok, chans), F32),
            pltpu.VMEM((CHUNK, chans), F32),
            pltpu.VMEM((2 * poles, tok), BF16),
            pltpu.VMEM((tok, 4 * poles), BF16),
            pltpu.VMEM((CHUNK, 4 * poles), BF16),
            pltpu.VMEM((2 * poles, CHUNK), BF16),
        ] + [sem] * 8,
        compiler_params=pltpu.CompilerParams(
            collective_id=0, has_side_effects=True, vmem_limit_bytes=48 * 1024 * 1024
        ),
    )(
        seq_feats, taps, pole_table.reshape(1, poles), mode_index, residues, skip.reshape(1, own)
    )


def solution(mesh):
    return jax.shard_map(
        body,
        mesh=mesh,
        in_specs=(
            P(("grp", "ctx"), None),
            P(),
            P(),
            P(("grp", "ctx"), None),
            P(("grp", "ctx"), None),
            P(("grp", "ctx")),
        ),
        out_specs=P(("grp", "ctx"), None),
        check_vma=False,
    )
```

profile of v0, /device:TPU:0, one launch (start us, length us, event | category | flops | bytes accessed | tf_op | source)
XLA Modules:
  0.0 25.5 jit_solution(2904882455874306834)
XLA Ops:
  0.0 0.0 copy-start.4
  0.0 0.0 copy-start.5
  0.0 0.7 %copy-done.4 = f32[64]{0:T(128)S(1)} copy-done((f32[64]{0:T(128)S(1)}, f32[64]{0:T(128)}, u32[]{:S(2)}) %copy-start.4) | copy-done | bytes 280
  0.7 0.0 copy-done.5
  0.7 0.0 copy-start
  0.7 1.1 %copy-done = bf16[512,768]{1,0:T(8,128)(2,1)S(1)} copy-done((bf16[512,768]{1,0:T(8,128)(2,1)S(1)}, bf16[512,768]{1,0:T(8,128)(2,1)}, u32[]{:S(2)}) %copy-start) | copy-done | bytes 786456
  1.8 0.0 copy-start.1
  1.8 0.7 %copy-done.1 = f32[7,768]{1,0:T(8,128)S(1)} copy-done((f32[7,768]{1,0:T(8,128)S(1)}, f32[7,768]{1,0:T(8,128)}, u32[]{:S(2)}) %copy-start.1) | copy-done | bytes 21528
  2.5 0.0 copy-start.2
  2.5 0.7 %copy-done.2 = s32[8,16]{1,0:T(8,128)S(1)} copy-done((s32[8,16]{1,0:T(8,128)S(1)}, s32[8,16]{1,0:T(8,128)}, u32[]{:S(2)}) %copy-start.2) | copy-done | bytes 536
  3.2 0.0 copy-start.3
  3.2 0.7 %copy-done.3 = f32[8,16]{1,0:T(8,128)S(1)} copy-done((f32[8,16]{1,0:T(8,128)S(1)}, f32[8,16]{1,0:T(8,128)}, u32[]{:S(2)}) %copy-start.3) | copy-done | bytes 536
  3.9 20.9 %shard_map.64 = bf16[512,256]{1,0:T(8,128)(2,1)S(1)} custom-call(bf16[512,768]{1,0:T(8,128)(2,1)S(1)} %copy-done, f32[7,768]{1,0:T(8,128)S(1)} %copy-done.1, f32[1,64]{1,0:T(1,128)S(1)} %bitcast.2, s32[8,16]{1,0:T(8,128)S(1)} %copy-done.2, f32[8,16]{1,0:T(8,128)S(1)} %copy-done.3, f32[1,8]{1,0:T(1,128)S(1)} %bitcast.3), custom_call_target="tpu_custom_call" | custom-call | tf_op jit(solution)/shard_map/pallas_call | solution.py:263
  24.8 0.7 %copy.8 = bf16[512,256]{1,0:T(8,128)(2,1)} copy(bf16[512,256]{1,0:T(8,128)(2,1)S(1)} %shard_map.64) | data formatting | bytes 524288
Async XLA Ops:
  0.0 0.7 %copy-start.4 = (f32[64]{0:T(128)S(1)}, f32[64]{0:T(128)}, u32[]{:S(2)}) copy-start(f32[64]{0:T(128)} %param.8) | copy-start | bytes 772
  0.0 0.7 %copy-start.5 = (f32[8]{0:T(128)S(1)}, f32[8]{0:T(128)}, u32[]{:S(2)}) copy-start(f32[8]{0:T(128)} %param.11) | copy-start | bytes 100
  0.7 1.1 %copy-start = (bf16[512,768]{1,0:T(8,128)(2,1)S(1)}, bf16[512,768]{1,0:T(8,128)(2,1)}, u32[]{:S(2)}) copy-start(bf16[512,768]{1,0:T(8,128)(2,1)} %x_ref.1) | copy-start | bytes 2359300
  1.8 0.7 %copy-start.1 = (f32[7,768]{1,0:T(8,128)S(1)}, f32[7,768]{1,0:T(8,128)}, u32[]{:S(2)}) copy-start(f32[7,768]{1,0:T(8,128)} %taps_ref.1) | copy-start | bytes 64516
  2.5 0.7 %copy-start.2 = (s32[8,16]{1,0:T(8,128)S(1)}, s32[8,16]{1,0:T(8,128)}, u32[]{:S(2)}) copy-start(s32[8,16]{1,0:T(8,128)} %mode_ref.1) | copy-start | bytes 1540
  3.2 0.7 %copy-start.3 = (f32[8,16]{1,0:T(8,128)S(1)}, f32[8,16]{1,0:T(8,128)}, u32[]{:S(2)}) copy-start(f32[8,16]{1,0:T(8,128)} %res_ref.1) | copy-start | bytes 1540
where the time goes:
time: 25.8 us; the launch traced here: 25.5 us
  Pallas kernels  20.9 us (81%)
  local copies, waits for them, and re-layouts  4.62 us (18%)
    pallas_call x1, Pallas kernels, body(): pl.pallas_call(functools.partial(kernel, outer, inner), out_shape=jax.Sha...  20.9 us
    unnamed x13, local copies, waits for them, and re-layouts  4.62 us

commit v1 on v0

v1 whole, which is shorter than its diff:
```python
import functools

import jax
import jax.numpy as jnp
from jax import lax
from jax.experimental import pallas as pl
from jax.experimental.pallas import tpu as pltpu
from jax.sharding import PartitionSpec as P

F32 = jnp.float32
BF16 = jnp.bfloat16
CHUNK = 32
ROWS = 64
GROUP = 8
COLS = 256
MESH = pl.DeviceIdType.MESH


def upper(value):
    return value.astype(BF16).astype(F32)


def paired(value, poles):
    high = upper(value)
    lane = lax.broadcasted_iota(jnp.int32, value.shape, 1)
    both = jnp.where(lane < poles, high, value - high).astype(BF16)
    return jnp.concatenate([both, both], axis=1)


def dot_last(left, right):
    return lax.dot_general(left, right, (((1,), (1,)), ((), ())), preferred_element_type=F32)


def kernel(
    outer, inner, x_hbm, taps_hbm, pole_hbm, mode_hbm, res_hbm, skip_hbm, out_ref,
    x_ref, taps_ref, pole_ref, mode_ref, res_ref, skip_ref, in_sems,
    halo, wall, wsend, state, landed, totals, turned, incoming,
    xs, gs, gb, grid, ys, qs, filt, acat, bcat, fcat, short,
    halo_send, halo_recv, w_send, w_recv, g_send, g_recv, s_send, s_recv, t_send, t_recv, x_send, x_recv,
):
    count = outer * inner
    operands = []
    for number, (source, target) in enumerate((
        (pole_hbm, pole_ref), (mode_hbm, mode_ref), (res_hbm, res_ref), (skip_hbm, skip_ref),
        (taps_hbm, taps_ref), (x_hbm, x_ref),
    )):
        operands.append(pltpu.make_async_copy(source, target, in_sems.at[number]))
        operands[-1].start()
    tok, width3 = x_ref.shape
    chans = width3 // 3
    ntaps = taps_ref.shape[0]
    poles = pole_ref.shape[1]
    own, modes = mode_ref.shape
    seq = tok * count
    nchunk = tok // CHUNK
    my_grp, my_ctx = lax.axis_index("grp"), lax.axis_index("ctx")
    me = my_grp * inner + my_ctx

    def wrapped(index, size):
        return jnp.where(index >= size, index - size, index)

    spans = inner // GROUP
    groups = outer * spans
    span, member = my_ctx // GROUP, lax.rem(my_ctx, GROUP)
    group = my_grp * spans + span
    share = chans // GROUP
    packed = share // 2

    def for_members(visit):
        for ahead in range(1, GROUP):
            peer = wrapped(member + ahead, GROUP)
            visit(peer, {"grp": my_grp, "ctx": span * GROUP + peer})

    def for_groups(visit):
        for ahead in range(outer):
            grp = wrapped(my_grp + ahead, outer)
            for further in range(1 if ahead == 0 else 0, spans):
                there = wrapped(span + further, spans)
                visit(grp * spans + there, {"grp": grp, "ctx": there * GROUP + member})

    def send(source, target, sent, received, place):
        pltpu.make_async_remote_copy(
            src_ref=source, dst_ref=target, send_sem=sent, recv_sem=received,
            device_id=place, device_id_type=MESH,
        ).start()

    def settle(ref, semaphore):
        pltpu.make_async_copy(ref, ref, semaphore).wait()

    behind = {
        "grp": jnp.where(my_ctx == 0, my_grp - 1, my_grp),
        "ctx": jnp.where(my_ctx == 0, inner - 1, my_ctx - 1),
    }
    barrier = pltpu.get_barrier_semaphore()

    def greet(peer, place):
        pl.semaphore_signal(barrier, inc=1, device_id=place, device_id_type=MESH)

    for_members(greet)
    for_groups(greet)

    @pl.when(me > 0)
    def _():
        greet(0, behind)

    for copy in operands[:4]:
        copy.wait()
    pole = jnp.concatenate([pole_ref[...], pole_ref[...]], axis=1)
    small = -2.0 / pole
    series = small * (1.0 + small * (0.5 + small * (1.0 / 6 + small * (1.0 / 24 + small * (
        1.0 / 120 + small * (1.0 / 720))))))
    energy = (jnp.exp(-2.0 * seq / pole) - 1.0) / series
    lane = lax.broadcasted_iota(jnp.int32, (own, 2 * poles), 1)
    entry = lax.rem(lane, poles)
    weight = jnp.zeros((own, 2 * poles), F32)
    for mode in range(modes):
        weight += jnp.where(mode_ref[:, mode : mode + 1] == entry, res_ref[:, mode : mode + 1], 0.0)
    weight = weight / jnp.sqrt(energy)
    diag = lax.broadcasted_iota(jnp.int32, (own, own), 0) == lax.broadcasted_iota(jnp.int32, (own, own), 1)
    skip_col = jnp.sum(jnp.where(diag, skip_ref[...], 0.0), axis=1, keepdims=True)
    wsend[...] = jnp.where(lane < poles, weight, jnp.where(lane == poles, skip_col, 0.0))
    wall[group, member] = wsend[...]

    grid[0:CHUNK] = jnp.zeros((CHUNK, nchunk, chans), F32)

    pl.semaphore_wait(barrier, GROUP - 1 + groups - 1 + jnp.where(me < count - 1, 1, 0))

    halo_copy = pltpu.make_async_remote_copy(
        src_ref=x_hbm.at[tok - 16 :], dst_ref=halo, send_sem=halo_send, recv_sem=halo_recv,
        device_id={
            "grp": wrapped(my_grp + jnp.where(my_ctx == inner - 1, 1, 0), outer),
            "ctx": wrapped(my_ctx + 1, inner),
        },
        device_id_type=MESH,
    )

    @pl.when(me < count - 1)
    def _():
        halo_copy.start()

    @pl.when(me == 0)
    def _():
        halo[...] = jnp.zeros_like(halo)

    def push_weight(peer, place):
        send(wsend, wall.at[group, member], w_send, w_recv, place)

    for_groups(push_weight)

    square = lax.broadcasted_iota(jnp.int32, (poles, poles), 0) == lax.broadcasted_iota(
        jnp.int32, (poles, poles), 1)
    column = jnp.sum(jnp.where(square, pole_ref[...], 0.0), axis=1, keepdims=True)

    def ending(length):
        back = (length - 1 - lax.broadcasted_iota(jnp.int32, (poles, length), 1)).astype(F32)
        table = jnp.exp(-back * (1.0 / column))
        high = upper(table)
        return jnp.concatenate([high.astype(BF16), (table - high).astype(BF16)], axis=0)

    def starting(length, first):
        ahead = (first + lax.broadcasted_iota(jnp.int32, (length, 2 * poles), 0)).astype(F32)
        table = jnp.exp(-ahead * (1.0 / pole))
        high = upper(table)
        return jnp.concatenate([high.astype(BF16), (table - high).astype(BF16)], axis=1)

    acat[...] = ending(tok)
    short[...] = ending(CHUNK)
    bcat[...] = starting(tok, 1)
    fcat[...] = starting(CHUNK, 0)

    def fir(block, col):
        rows = xs[pl.ds(pl.multiple_of(block * ROWS, ROWS), ROWS + 8), col : col + COLS]
        total = jnp.zeros((ROWS, COLS), F32)
        for tap in range(ntaps):
            total += taps_ref[tap : tap + 1, col : col + COLS] * rows[8 - tap : 8 - tap + ROWS]
        return total

    def gate(block, carry):
        place = pl.ds(pl.multiple_of(block * ROWS, ROWS), ROWS)
        for col in range(0, chans, COLS):
            low = (fir(block, chans + col) * fir(block, 2 * chans + col)).astype(BF16)
            gb[place, col : col + COLS] = low
            wide = low.astype(F32)
            for part in range(0, COLS, 128):
                gs[(col + part) // 128, place, :] = wide[:, part : part + 128]
        return carry

    for copy in operands[4:]:
        copy.wait()
    xs[8:, :] = x_ref[...].astype(F32)
    lax.fori_loop(1, tok // ROWS, gate, 0)

    @pl.when(me > 0)
    def _():
        halo_copy.wait_recv()

    xs[0:8, :] = halo[...].astype(F32)[8:16]
    gate(0, 0)

    ends = jnp.dot(acat[...], gb[...], preferred_element_type=F32).T
    ends = ends + pltpu.roll(ends, poles, 1)
    left_lanes = lax.broadcasted_iota(jnp.int32, (packed, 2 * poles), 1) < poles
    for index in range(GROUP):
        start = index * share
        state[index] = jnp.where(
            left_lanes, ends[start : start + packed], ends[start + packed : start + share])
    landed[member] = state[member]

    def push_state(peer, place):
        send(state.at[peer], landed.at[member], s_send, s_recv, place)

    for_members(push_state)

    settle(wall.at[0 : groups - 1, 0], w_recv)

    def push_gathered(peer, place):
        send(wall.at[:, member], wall.at[:, member], g_send, g_recv, place)

    for_members(push_gathered)

    def query(block, carry):
        place = pl.ds(pl.multiple_of(block * ROWS, ROWS), ROWS)
        for col in range(0, chans, COLS):
            qs[place, col : col + COLS] = fir(block, col)
        return carry

    lax.fori_loop(0, tok // ROWS, query, 0)

    for pos in range(CHUNK):
        for col in range(0, chans, 128):
            grid[CHUNK + pos, :, col : col + 128] = gs[col // 128, pl.ds(pos, nchunk, stride=CHUNK), :]

    settle(landed.at[0 : GROUP - 1], s_recv)
    jump = jnp.exp(-float(tok) / pole)
    total = landed[0]
    for source in range(1, GROUP):
        total = total * jump + landed[source]
    totals[group] = total

    def push_total(peer, place):
        send(totals.at[group], totals.at[group], t_send, t_recv, place)

    for_groups(push_total)

    settle(wall.at[:, 0 : GROUP - 1], g_recv)
    lane_all = lax.broadcasted_iota(jnp.int32, (chans, 2 * poles), 1)
    gathered = wall[...].reshape(chans, 2 * poles)
    twice = jnp.where(lane_all < poles, gathered, pltpu.roll(gathered, poles, 1))
    across = gathered.T
    by_pole = across[0:poles]
    first_row = lax.broadcasted_iota(jnp.int32, (CHUNK, chans), 0) == 0
    filt[...] = dot_last(fcat[...], paired(twice, poles)) + jnp.where(
        first_row, across[poles : poles + 1], 0.0)

    def within(pos, carry):
        for col in range(0, chans, 128):
            total = jnp.zeros((nchunk, 128), F32)
            for lag in range(CHUNK):
                total += filt[lag : lag + 1, col : col + 128] * grid[CHUNK + pos - lag, :, col : col + 128]
            ys[col // 128, pl.ds(pos, nchunk, stride=CHUNK), :] = total
        return carry

    lax.fori_loop(0, CHUNK, within, 0)

    settle(totals.at[0 : groups - 1], t_recv)
    leap = jnp.exp(-float(tok * GROUP) / pole)
    running = jnp.zeros((packed, 2 * poles), F32)
    for source in range(groups - 1):
        running = jnp.where(source < group, running * leap + totals[source], running)
    for source in range(GROUP):
        turned[source] = running
        running = running * jump + landed[source]
    incoming[member] = turned[member]

    def push_turned(peer, place):
        send(turned.at[peer], incoming.at[member], x_send, x_recv, place)

    for_members(push_turned)

    hop = jnp.exp(-float(CHUNK) / column)

    def between(chunk, carried):
        place = pl.ds(pl.multiple_of(chunk * CHUNK, CHUNK), CHUNK)
        high = carried.astype(BF16)
        low = (carried - high.astype(F32)).astype(BF16)
        stack = jnp.concatenate([high, low, high, low], axis=0)
        entering = jnp.dot(bcat[0:CHUNK, :], stack, preferred_element_type=F32)
        for col in range(0, chans, 128):
            ys[col // 128, place, :] += entering[:, col : col + 128]
        fresh = jnp.dot(short[...], gb[place, :], preferred_element_type=F32)
        return carried * hop + by_pole * (fresh[0:poles] + fresh[poles:])

    lax.fori_loop(0, nchunk, between, jnp.zeros((poles, chans), F32))

    settle(incoming.at[0 : GROUP - 1], x_recv)
    parts = []
    for index in range(GROUP):
        held = incoming[index]
        swapped = pltpu.roll(held, poles, 1)
        parts += [jnp.where(left_lanes, held, swapped), jnp.where(left_lanes, swapped, held)]
    stack = paired(jnp.concatenate(parts, axis=0) * twice, poles)
    for row in range(0, tok, 128):
        conv = dot_last(bcat[row : row + 128, :], stack)
        for col in range(0, chans, 128):
            mixed = conv[:, col : col + 128] + ys[col // 128, row : row + 128, :]
            out_ref[row : row + 128, col : col + 128] = (
                qs[row : row + 128, col : col + 128] * mixed).astype(BF16)

    @pl.when(me < count - 1)
    def _():
        halo_copy.wait_send()

    settle(wall.at[0 : groups - 1, 0], w_send)
    settle(wall.at[:, 0 : GROUP - 1], g_send)
    settle(landed.at[0 : GROUP - 1], s_send)
    settle(totals.at[0 : groups - 1], t_send)
    settle(incoming.at[0 : GROUP - 1], x_send)


def body(seq_feats, taps, pole_table, mode_index, residues, skip):
    tok, width3 = seq_feats.shape
    chans = width3 // 3
    outer = lax.axis_size("grp")
    inner = lax.axis_size("ctx")
    count = outer * inner
    poles = pole_table.shape[0]
    own = mode_index.shape[0]
    nchunk = tok // CHUNK
    groups, packed = count // GROUP, chans // GROUP // 2
    vmem = pl.BlockSpec(memory_space=pltpu.VMEM)
    sem = pltpu.SemaphoreType.DMA
    return pl.pallas_call(
        functools.partial(kernel, outer, inner),
        out_shape=jax.ShapeDtypeStruct((tok, chans), BF16),
        in_specs=[pl.BlockSpec(memory_space=pltpu.HBM)] * 6,
        out_specs=vmem,
        scratch_shapes=[
            pltpu.VMEM((tok, width3), BF16),
            pltpu.VMEM(taps.shape, F32),
            pltpu.VMEM((1, poles), F32),
            pltpu.VMEM(mode_index.shape, jnp.int32),
            pltpu.VMEM(residues.shape, F32),
            pltpu.VMEM((1, own), F32),
            sem((6,)),
            pltpu.VMEM((16, width3), BF16),
            pltpu.VMEM((groups, GROUP, own, 2 * poles), F32),
            pltpu.VMEM((own, 2 * poles), F32),
            pltpu.VMEM((GROUP, packed, 2 * poles), F32),
            pltpu.VMEM((GROUP, packed, 2 * poles), F32),
            pltpu.VMEM((groups, packed, 2 * poles), F32),
            pltpu.VMEM((GROUP, packed, 2 * poles), F32),
            pltpu.VMEM((GROUP, packed, 2 * poles), F32),
            pltpu.VMEM((tok + 8, width3), F32),
            pltpu.VMEM((chans // 128, tok, 128), F32),
            pltpu.VMEM((tok, chans), BF16),
            pltpu.VMEM((2 * CHUNK, nchunk, chans), F32),
            pltpu.VMEM((chans // 128, tok, 128), F32),
            pltpu.VMEM((tok, chans), F32),
            pltpu.VMEM((CHUNK, chans), F32),
            pltpu.VMEM((2 * poles, tok), BF16),
            pltpu.VMEM((tok, 4 * poles), BF16),
            pltpu.VMEM((CHUNK, 4 * poles), BF16),
            pltpu.VMEM((2 * poles, CHUNK), BF16),
        ] + [sem] * 12,
        compiler_params=pltpu.CompilerParams(
            collective_id=0, has_side_effects=True, vmem_limit_bytes=64 * 1024 * 1024
        ),
    )(
        seq_feats, taps, pole_table.reshape(1, poles), mode_index, residues, skip.reshape(1, own)
    )


def solution(mesh):
    return jax.shard_map(
        body,
        mesh=mesh,
        in_specs=(
            P(("grp", "ctx"), None),
            P(),
            P(),
            P(("grp", "ctx"), None),
            P(("grp", "ctx"), None),
            P(("grp", "ctx")),
        ),
        out_specs=P(("grp", "ctx"), None),
        check_vma=False,
    )
```

time: 25.8 us -> 22 us (0.85)
  local copies, waits for them, and re-layouts: 4.62 us -> 1.67 us
  Pallas kernels: 20.9 us -> 20.2 us
    unnamed x13 -> x1, local copies, waits for them, and re-layouts: 4.62 us -> 1.67 us
    pallas_call x1, Pallas kernels: 20.9 us -> 20.2 us  [body(): pl.pallas_call(functools.partial(kernel, outer, inner), out_shape=jax.Sha...]
where the time goes in v1:
time: 22 us; the launch traced here: 21.8 us
  Pallas kernels  20.2 us (92%)
  local copies, waits for them, and re-layouts  1.67 us (8%)
    pallas_call x1, Pallas kernels, body(): pl.pallas_call(functools.partial(kernel, outer, inner), out_shape=jax.Sha...  20.2 us
    unnamed x1, local copies, waits for them, and re-layouts  1.67 us

profile of v1, /device:TPU:0, one launch (start us, length us, event | category | flops | bytes accessed | tf_op | source)
XLA Modules:
  0.0 21.8 jit_solution(15825473951468155280)
XLA Ops:
  0.0 20.2 %shard_map.64 = bf16[512,256]{1,0:T(8,128)(2,1)} custom-call(bf16[512,768]{1,0:T(8,128)(2,1)} %x_hbm.1, f32[7,768]{1,0:T(8,128)} %taps_hbm.1, f32[1,64]{1,0:T(1,128)} %bitcast.2, s32[8,16]{1,0:T(8,128)} %mode_hbm.1, f32[8,16]{1,0:T(8,128)} %res_hbm.1, f32[1,8]{1,0:T(1,128)} %bitcast.3), custom_call_target="tpu_custom_call" | custom-call | tf_op jit(solution)/shard_map/pallas_call | solution.py:332
  20.2 1.7 %copy.8 = bf16[512,256]{1,0:T(8,128)(2,1)} copy(bf16[512,256]{1,0:T(8,128)(2,1)} %shard_map.64) | data formatting | bytes 524288

commit v2 on v1

--- a/solution.py
+++ b/solution.py
@@ -32,7 +32,7 @@
 
 
 def kernel(
-    outer, inner, x_hbm, taps_hbm, pole_hbm, mode_hbm, res_hbm, skip_hbm, out_ref,
+    outer, inner, x_hbm, taps_hbm, pole_hbm, mode_hbm, res_hbm, skip_hbm, out_hbm, out_ref, out_sems,
     x_ref, taps_ref, pole_ref, mode_ref, res_ref, skip_ref, in_sems,
     halo, wall, wsend, state, landed, totals, turned, incoming,
     xs, gs, gb, grid, ys, qs, filt, acat, bcat, fcat, short,
@@ -121,7 +121,28 @@
     wsend[...] = jnp.where(lane < poles, weight, jnp.where(lane == poles, skip_col, 0.0))
     wall[group, member] = wsend[...]
 
-    grid[0:CHUNK] = jnp.zeros((CHUNK, nchunk, chans), F32)
+
+    square = lax.broadcasted_iota(jnp.int32, (poles, poles), 0) == lax.broadcasted_iota(
+        jnp.int32, (poles, poles), 1)
+    column = jnp.sum(jnp.where(square, pole_ref[...], 0.0), axis=1, keepdims=True)
+
+    def ending(length):
+        back = (length - 1 - lax.broadcasted_iota(jnp.int32, (poles, length), 1)).astype(F32)
+        table = jnp.exp(-back * (1.0 / column))
+        high = upper(table)
+        return jnp.concatenate([high.astype(BF16), (table - high).astype(BF16)], axis=0)
+
+    def starting(length, first):
+        ahead = (first + lax.broadcasted_iota(jnp.int32, (length, 2 * poles), 0)).astype(F32)
+        table = jnp.exp(-ahead * (1.0 / pole))
+        high = upper(table)
+        return jnp.concatenate([high.astype(BF16), (table - high).astype(BF16)], axis=1)
+
+    acat[...] = ending(tok)
+
+    for copy in operands[4:]:
+        copy.wait()
+    xs[8:, chans:] = x_ref[:, chans:].astype(F32)
 
     pl.semaphore_wait(barrier, GROUP - 1 + groups - 1 + jnp.where(me < count - 1, 1, 0))
 
@@ -146,27 +167,6 @@
         send(wsend, wall.at[group, member], w_send, w_recv, place)
 
     for_groups(push_weight)
-
-    square = lax.broadcasted_iota(jnp.int32, (poles, poles), 0) == lax.broadcasted_iota(
-        jnp.int32, (poles, poles), 1)
-    column = jnp.sum(jnp.where(square, pole_ref[...], 0.0), axis=1, keepdims=True)
-
-    def ending(length):
-        back = (length - 1 - lax.broadcasted_iota(jnp.int32, (poles, length), 1)).astype(F32)
-        table = jnp.exp(-back * (1.0 / column))
-        high = upper(table)
-        return jnp.concatenate([high.astype(BF16), (table - high).astype(BF16)], axis=0)
-
-    def starting(length, first):
-        ahead = (first + lax.broadcasted_iota(jnp.int32, (length, 2 * poles), 0)).astype(F32)
-        table = jnp.exp(-ahead * (1.0 / pole))
-        high = upper(table)
-        return jnp.concatenate([high.astype(BF16), (table - high).astype(BF16)], axis=1)
-
-    acat[...] = ending(tok)
-    short[...] = ending(CHUNK)
-    bcat[...] = starting(tok, 1)
-    fcat[...] = starting(CHUNK, 0)
 
     def fir(block, col):
         rows = xs[pl.ds(pl.multiple_of(block * ROWS, ROWS), ROWS + 8), col : col + COLS]
@@ -185,9 +185,6 @@
                 gs[(col + part) // 128, place, :] = wide[:, part : part + 128]
         return carry
 
-    for copy in operands[4:]:
-        copy.wait()
-    xs[8:, :] = x_ref[...].astype(F32)
     lax.fori_loop(1, tok // ROWS, gate, 0)
 
     @pl.when(me > 0)
@@ -217,6 +214,12 @@
         send(wall.at[:, member], wall.at[:, member], g_send, g_recv, place)
 
     for_members(push_gathered)
+
+    short[...] = ending(CHUNK)
+    bcat[...] = starting(tok, 1)
+    fcat[...] = starting(CHUNK, 0)
+    grid[0:CHUNK] = jnp.zeros((CHUNK, nchunk, chans), F32)
+    xs[8:, 0:chans] = x_ref[:, 0:chans].astype(F32)
 
     def query(block, carry):
         place = pl.ds(pl.multiple_of(block * ROWS, ROWS), ROWS)
@@ -299,12 +302,16 @@
         swapped = pltpu.roll(held, poles, 1)
         parts += [jnp.where(left_lanes, held, swapped), jnp.where(left_lanes, swapped, held)]
     stack = paired(jnp.concatenate(parts, axis=0) * twice, poles)
+    results = []
     for row in range(0, tok, 128):
         conv = dot_last(bcat[row : row + 128, :], stack)
         for col in range(0, chans, 128):
             mixed = conv[:, col : col + 128] + ys[col // 128, row : row + 128, :]
             out_ref[row : row + 128, col : col + 128] = (
                 qs[row : row + 128, col : col + 128] * mixed).astype(BF16)
+        results.append(pltpu.make_async_copy(
+            out_ref.at[row : row + 128], out_hbm.at[row : row + 128], out_sems.at[row // 128]))
+        results[-1].start()
 
     @pl.when(me < count - 1)
     def _():
@@ -315,6 +322,8 @@
     settle(landed.at[0 : GROUP - 1], s_send)
     settle(totals.at[0 : groups - 1], t_send)
     settle(incoming.at[0 : GROUP - 1], x_send)
+    for copy in results:
+        copy.wait()
 
 
 def body(seq_feats, taps, pole_table, mode_index, residues, skip):
@@ -327,14 +336,15 @@
     own = mode_index.shape[0]
     nchunk = tok // CHUNK
     groups, packed = count // GROUP, chans // GROUP // 2
-    vmem = pl.BlockSpec(memory_space=pltpu.VMEM)
     sem = pltpu.SemaphoreType.DMA
     return pl.pallas_call(
         functools.partial(kernel, outer, inner),
         out_shape=jax.ShapeDtypeStruct((tok, chans), BF16),
         in_specs=[pl.BlockSpec(memory_space=pltpu.HBM)] * 6,
-        out_specs=vmem,
+        out_specs=pl.BlockSpec(memory_space=pltpu.HBM),
         scratch_shapes=[
+            pltpu.VMEM((tok, chans), BF16),
+            sem((tok // 128,)),
             pltpu.VMEM((tok, width3), BF16),
             pltpu.VMEM(taps.shape, F32),
             pltpu.VMEM((1, poles), F32),

time: 22 us -> 22 us (level)
  no operation moved by 1% of the time
where the time goes in v2:
time: 22 us; the launch traced here: 21.9 us
  Pallas kernels  20.2 us (92%)
  local copies, waits for them, and re-layouts  1.67 us (8%)
    pallas_call x1, Pallas kernels, body(): pl.pallas_call(functools.partial(kernel, outer, inner), out_shape=jax.Sha...  20.2 us
    unnamed x1, local copies, waits for them, and re-layouts  1.67 us

profile of v2, /device:TPU:0, one launch (start us, length us, event | category | flops | bytes accessed | tf_op | source)
XLA Modules:
  0.0 21.9 jit_solution(12171891583937433856)
XLA Ops:
  0.0 20.2 %shard_map.64 = bf16[512,256]{1,0:T(8,128)(2,1)} custom-call(bf16[512,768]{1,0:T(8,128)(2,1)} %x_hbm.1, f32[7,768]{1,0:T(8,128)} %taps_hbm.1, f32[1,64]{1,0:T(1,128)} %bitcast.2, s32[8,16]{1,0:T(8,128)} %mode_hbm.1, f32[8,16]{1,0:T(8,128)} %res_hbm.1, f32[1,8]{1,0:T(1,128)} %bitcast.3), custom_call_target="tpu_custom_call" | custom-call | tf_op jit(solution)/shard_map/pallas_call | solution.py:340
  20.2 1.7 %copy.8 = bf16[512,256]{1,0:T(8,128)(2,1)} copy(bf16[512,256]{1,0:T(8,128)(2,1)} %shard_map.64) | data formatting | bytes 524288

commit v3 on v2

--- a/solution.py
+++ b/solution.py
@@ -39,13 +39,6 @@
     halo_send, halo_recv, w_send, w_recv, g_send, g_recv, s_send, s_recv, t_send, t_recv, x_send, x_recv,
 ):
     count = outer * inner
-    operands = []
-    for number, (source, target) in enumerate((
-        (pole_hbm, pole_ref), (mode_hbm, mode_ref), (res_hbm, res_ref), (skip_hbm, skip_ref),
-        (taps_hbm, taps_ref), (x_hbm, x_ref),
-    )):
-        operands.append(pltpu.make_async_copy(source, target, in_sems.at[number]))
-        operands[-1].start()
     tok, width3 = x_ref.shape
     chans = width3 // 3
     ntaps = taps_ref.shape[0]
@@ -96,13 +89,20 @@
     def greet(peer, place):
         pl.semaphore_signal(barrier, inc=1, device_id=place, device_id_type=MESH)
 
+    for_groups(greet)
     for_members(greet)
-    for_groups(greet)
 
     @pl.when(me > 0)
     def _():
         greet(0, behind)
 
+    operands = []
+    for number, (source, target) in enumerate((
+        (pole_hbm, pole_ref), (mode_hbm, mode_ref), (res_hbm, res_ref), (skip_hbm, skip_ref),
+        (taps_hbm, taps_ref), (x_hbm, x_ref),
+    )):
+        operands.append(pltpu.make_async_copy(source, target, in_sems.at[number]))
+        operands[-1].start()
     for copy in operands[:4]:
         copy.wait()
     pole = jnp.concatenate([pole_ref[...], pole_ref[...]], axis=1)

time: 22 us -> 22 us (level)
  no operation moved by 1% of the time
where the time goes in v3:
time: 22 us; the launch traced here: 21.9 us
  Pallas kernels  20.2 us (92%)
  local copies, waits for them, and re-layouts  1.67 us (8%)
    pallas_call x1, Pallas kernels, body(): pl.pallas_call(functools.partial(kernel, outer, inner), out_shape=jax.Sha...  20.2 us
    unnamed x1, local copies, waits for them, and re-layouts  1.67 us

profile of v3, /device:TPU:0, one launch (start us, length us, event | category | flops | bytes accessed | tf_op | source)
XLA Modules:
  0.0 21.9 jit_solution(12579364377230177633)
XLA Ops:
  0.0 20.2 %shard_map.64 = bf16[512,256]{1,0:T(8,128)(2,1)} custom-call(bf16[512,768]{1,0:T(8,128)(2,1)} %x_hbm.1, f32[7,768]{1,0:T(8,128)} %taps_hbm.1, f32[1,64]{1,0:T(1,128)} %bitcast.2, s32[8,16]{1,0:T(8,128)} %mode_hbm.1, f32[8,16]{1,0:T(8,128)} %res_hbm.1, f32[1,8]{1,0:T(1,128)} %bitcast.3), custom_call_target="tpu_custom_call" | custom-call | tf_op jit(solution)/shard_map/pallas_call | solution.py:340
  20.2 1.7 %copy.8 = bf16[512,256]{1,0:T(8,128)(2,1)} copy(bf16[512,256]{1,0:T(8,128)(2,1)} %shard_map.64) | data formatting | bytes 524288
